TPU v7x, 32 devices: a whole 2x2x4 slice. The times are simulated.
32 devices in a mesh: grp: 1, ev: 32 (over z, y, x, core).
Axes of the slice: x: 2, y: 2, z: 4, core: 2. Of those that a mesh axis runs over, the one named last changes fastest.
Arguments:
- windows: bfloat16 [256, 3, 64, 1024], P(('grp', 'ev')), may hold values from -400 to 400, as said below
- rotation: bfloat16 [256, 3, 64], P(('grp', 'ev')), may hold values from -3 to 3
- source_inverse: bfloat16 [256, 1024], P(('grp', 'ev')), may hold values from -3.4 to 3.4
- send_rows: int32 [1024, 64], P(('grp', 'ev')), may hold values from 0 to 511, as said below
- tile_station: int32 [2048], P(('grp', 'ev')), may hold values from 0 to 63, as said below
- tile_count: int32 [2048], P(('grp', 'ev')), may hold values from 16 to 128
- pair_rows: int32 [2, 262144], P(None, ('grp', 'ev')), may hold values from 0 to 2047, as said below
Outputs:
- correlation: float32 [262144, 255], P(('grp', 'ev'))
Inputs may be any that keep to these rules, and one draw needn't show every extreme that they name: Each event's windows carry a scale of their own, and each station's another. `send_rows`: row j of the block of device o names the rows of device o sent to device j, each as local event times 64 plus station, with the station of the tile whose residue matches the receiving slot (o * 64 + k) mod 64. `tile_station`: tile t of a device is fed by received slots r with r mod 64 = t mod 64, all at the tile's station. `pair_rows`: entries count the rows a device receives by sending device then slot; both members of a slot lie at its tile's station.
All inputs are finite; a program needn't handle non-finite values.
Results may differ from a plain program's by a relative error of at most 0.007.
Values may be sent and summed in bfloat16 or wider, within the bound.
A program may use at most 64 MiB of HBM per device.

v0:
```python
from functools import partial
import math

import jax
import jax.numpy as jnp
from jax import lax
from jax.sharding import PartitionSpec as P

LAGS = 255


epsilon = 1e-06


def spectral_table(length):
    half_len = length // 2
    samples = jnp.arange(length, dtype=jnp.int32)[:, None]
    frequency = jnp.arange(half_len, dtype=jnp.int32)[None, :]
    angles = (samples * frequency % length).astype(jnp.float32) * (2.0 * math.pi / length)
    factor = 1.0 / math.sqrt(length)
    return jnp.concatenate([jnp.cos(angles) * factor, -jnp.sin(angles) * factor], axis=1).astype(
        jnp.bfloat16
    )


def lag_table(length, lag_count):
    half_len = length // 2
    frequency = jnp.arange(half_len, dtype=jnp.int32)[:, None]
    shifts = jnp.arange(lag_count, dtype=jnp.int32)[None, :] - lag_count // 2
    angles = (frequency * shifts % length).astype(jnp.float32) * (2.0 * math.pi / length)
    factor = 1.0 / math.sqrt(half_len)
    return jnp.concatenate([jnp.cos(angles) * factor, -jnp.sin(angles) * factor], axis=0).astype(
        jnp.bfloat16
    )


def event_spectra(windows, rotation, source_inverse, dft_table):
    half_len = dft_table.shape[1] // 2
    transverse = jnp.sum(
        rotation.astype(jnp.float32)[..., None] * windows.astype(jnp.float32), axis=1
    ).astype(jnp.bfloat16)
    events, stations, length = transverse.shape
    spectrum = jnp.dot(
        transverse.reshape(events * stations, length), dft_table, preferred_element_type=jnp.float32
    )
    spectrum = spectrum.reshape(events, stations, length)
    filter_gain = source_inverse.astype(jnp.float32)[:, None, :]
    real_in, imag_in = (spectrum[..., :half_len], spectrum[..., half_len:])
    real_gain, imag_gain = (filter_gain[..., :half_len], filter_gain[..., half_len:])
    return jnp.concatenate(
        [real_in * real_gain - imag_in * imag_gain, real_in * imag_gain + imag_in * real_gain],
        axis=-1,
    )


def correlate_group(spectra, lag_tab, tile_pairs, pieces):
    first_rows, second_rows, weights, counts = pieces
    half_len = spectra.shape[1] // 2
    first_spec = spectra[first_rows].astype(jnp.float32)
    second_spec = spectra[second_rows].astype(jnp.float32)
    first_re, first_im = (first_spec[:, :half_len], first_spec[:, half_len:])
    second_re, second_im = (second_spec[:, :half_len], second_spec[:, half_len:])
    row_weight = jnp.repeat(weights, tile_pairs, axis=0)
    cross_spec = jnp.concatenate(
        [
            (first_re * second_re + first_im * second_im) * row_weight,
            (first_im * second_re - first_re * second_im) * row_weight,
        ],
        axis=1,
    ).astype(jnp.bfloat16)
    lagged = jnp.dot(cross_spec, lag_tab, preferred_element_type=jnp.float32)
    live_rows = jnp.arange(lagged.shape[0], dtype=jnp.int32) % tile_pairs < jnp.repeat(
        counts, tile_pairs
    )
    return jnp.where(live_rows[:, None], lagged, jnp.zeros_like(lagged))


def shards(windows, rotation, source_inverse, send_rows, tile_station, tile_count, pair_rows):
    ev_dev, components, stations, length = windows.shape
    half_len = length // 2
    owners = lax.axis_size("ev")
    dft_table = spectral_table(length)
    deconvolved = event_spectra(windows, rotation, source_inverse, dft_table)
    local_power = jnp.sum(
        deconvolved[..., :half_len] ** 2 + deconvolved[..., half_len:] ** 2, axis=0
    )
    power_sum = lax.psum(local_power, "ev")
    weight = 1.0 / (power_sum / (ev_dev * owners) + epsilon)
    capacity = send_rows.shape[1]
    slot_total = owners * capacity
    own_rows = deconvolved.astype(jnp.bfloat16).reshape(ev_dev * stations, length)
    received = lax.all_to_all(own_rows[send_rows], "ev", split_axis=0, concat_axis=0, tiled=True)
    received = received.reshape(slot_total, length)
    tiles_dev = tile_station.shape[0]
    tile_pairs = pair_rows.shape[1] // tiles_dev
    onehot = (tile_station[:, None] == jnp.arange(stations, dtype=jnp.int32)[None, :]).astype(
        jnp.float32
    )
    tile_weight = jnp.dot(onehot, weight, precision=lax.Precision.HIGHEST)
    groups = tiles_dev // 4
    group_rows = 4 * tile_pairs
    correlate = partial(correlate_group, received, lag_table(length, LAGS), tile_pairs)
    result = lax.map(
        correlate,
        (
            pair_rows[0].reshape(groups, group_rows),
            pair_rows[1].reshape(groups, group_rows),
            tile_weight.reshape(groups, 4, half_len),
            tile_count.reshape(groups, 4),
        ),
    )
    return result.reshape(groups * group_rows, LAGS)


def solution(mesh):
    in_specs = (
        P(("grp", "ev"), None, None, None),
        P(("grp", "ev"), None, None),
        P(("grp", "ev"), None),
        P(("grp", "ev"), None),
        P(("grp", "ev")),
        P(("grp", "ev")),
        P(None, ("grp", "ev")),
    )
    out_specs = P(("grp", "ev"), None)
    return jax.shard_map(shards, mesh=mesh, in_specs=in_specs, out_specs=out_specs, check_vma=False)
```

profile of v0, /device:TPU:7, one launch (start us, length us, event | category | flops | bytes accessed | tf_op | source)
XLA Modules:
  0.0 417.6 jit_solution(10348635386327450920)
XLA Ops:
  6.5 8.6 %multiply_convert_fusion = (bf16[1024,512]{1,0:T(8,128)(2,1)S(1)}, bf16[1024,512]{1,0:T(8,128)(2,1)S(1)}) fusion(), kind=kLoop, calls=%fused_computation.38 | loop fusion | flops 9961472 | bytes 2097152 | tf_op jit(solution)/shard_map/convert.10
  20.5 9.7 %gather_fusion.2 = bf16[2048,1024]{1,0:T(8,128)(2,1)} fusion(bf16[512,1024]{1,0:T(8,128)(2,1)S(1)} %pad_maximum_fusion, s32[2048]{0:T(1024)S(1)} %broadcast_clamp_fusion), kind=kCustom, calls=%fused_computation.2 | custom fusion | bytes 8396800 | tf_op jit(solution)/shard_map/gather | solution.py:92
  30.1 6.4 %all-to-all-start = ((bf16[32,64,1024]{2,1,0:T(8,128)(2,1)}), bf16[32,64,1024]{2,1,0:T(8,128)(2,1)}, u32[]{:S(2)}, u32[]{:S(2)}) async-start(bf16[32,64,1024]{2,1,0:T(8,128)(2,1)} %bitcast.58), calls=%async_computation | async-start | bytes 8388608 | tf_op jit(solution)/shard_map/all_to_all | solution.py:92
  40.8 148.5 %all-reduce.2.cloned.1.call-done = f32[64,512]{1,0:T(8,128)} async-done(((f32[64,512]{1,0:T(8,128)}), f32[64,512]{1,0:T(8,128)}) %all-reduce.2.cloned.1.call-update) | async-done | bytes 131088 | tf_op jit(solution)/shard_map/psum | solution.py:87
  190.5 220.2 %while.12 = (s32[]{:T(128)}, f32[16,512,255]{2,1,0:T(8,128)}, s32[16,4]{1,0:T(8,128)S(1)}, s32[16,512]{1,0:T(8,128)S(1)}, bf16[2048,1024]{1,0:T(8,128)(2,1)}, /*...) while((s32[]{:T(128)}, f32[16,512,255]{2,1,0:T(8,128)}, ...), condition=%wide.region_4.5_spmd, body=%wide.region_3.4_spmd.sunk | while | flops 273293312 | bytes 19963572 | solution.py:103
  204.3 5.5 %gather_fusion = bf16[512,1024]{1,0:T(8,128)(2,1)S(1)} fusion(bf16[2048,1024]{1,0:T(8,128)(2,1)} %get-tuple-element.218, s32[1024]{0:T(1024)S(1)} %pad_clamp_fusion.4), kind=kCustom, calls=%fused_computation.1.clone.1 | custom fusion | bytes 2099200 | tf_op jit(solution)/shard_map/while/body/eval_jaxpr/gather | solution.py:60
  210.1 5.5 %gather_fusion.1 = bf16[512,1024]{1,0:T(8,128)(2,1)S(1)} fusion(bf16[2048,1024]{1,0:T(8,128)(2,1)} %get-tuple-element.218, s32[1024]{0:T(1024)S(1)} %pad_clamp_fusion.5), kind=kCustom, calls=%fused_computation.clone.1 | custom fusion | bytes 2099200 | tf_op jit(solution)/shard_map/while/body/eval_jaxpr/gather | solution.py:59
  231.9 5.5 %gather_fusion = bf16[512,1024]{1,0:T(8,128)(2,1)S(1)} fusion(bf16[2048,1024]{1,0:T(8,128)(2,1)} %get-tuple-element.218, s32[1024]{0:T(1024)S(1)} %pad_clamp_fusion.4), kind=kCustom, calls=%fused_computation.1.clone.1 | custom fusion | bytes 2099200 | tf_op jit(solution)/shard_map/while/body/eval_jaxpr/gather | solution.py:60
  237.6 5.5 %gather_fusion.1 = bf16[512,1024]{1,0:T(8,128)(2,1)S(1)} fusion(bf16[2048,1024]{1,0:T(8,128)(2,1)} %get-tuple-element.218, s32[1024]{0:T(1024)S(1)} %pad_clamp_fusion.5), kind=kCustom, calls=%fused_computation.clone.1 | custom fusion | bytes 2099200 | tf_op jit(solution)/shard_map/while/body/eval_jaxpr/gather | solution.py:59
  245.6 5.5 %gather_fusion = bf16[512,1024]{1,0:T(8,128)(2,1)S(1)} fusion(bf16[2048,1024]{1,0:T(8,128)(2,1)} %get-tuple-element.218, s32[1024]{0:T(1024)S(1)} %pad_clamp_fusion.4), kind=kCustom, calls=%fused_computation.1.clone.1 | custom fusion | bytes 2099200 | tf_op jit(solution)/shard_map/while/body/eval_jaxpr/gather | solution.py:60
  251.3 5.5 %gather_fusion.1 = bf16[512,1024]{1,0:T(8,128)(2,1)S(1)} fusion(bf16[2048,1024]{1,0:T(8,128)(2,1)} %get-tuple-element.218, s32[1024]{0:T(1024)S(1)} %pad_clamp_fusion.5), kind=kCustom, calls=%fused_computation.clone.1 | custom fusion | bytes 2099200 | tf_op jit(solution)/shard_map/while/body/eval_jaxpr/gather | solution.py:59
  259.4 5.5 %gather_fusion = bf16[512,1024]{1,0:T(8,128)(2,1)S(1)} fusion(bf16[2048,1024]{1,0:T(8,128)(2,1)} %get-tuple-element.218, s32[1024]{0:T(1024)S(1)} %pad_clamp_fusion.4), kind=kCustom, calls=%fused_computation.1.clone.1 | custom fusion | bytes 2099200 | tf_op jit(solution)/shard_map/while/body/eval_jaxpr/gather | solution.py:60
  265.1 5.5 %gather_fusion.1 = bf16[512,1024]{1,0:T(8,128)(2,1)S(1)} fusion(bf16[2048,1024]{1,0:T(8,128)(2,1)} %get-tuple-element.218, s32[1024]{0:T(1024)S(1)} %pad_clamp_fusion.5), kind=kCustom, calls=%fused_computation.clone.1 | custom fusion | bytes 2099200 | tf_op jit(solution)/shard_map/while/body/eval_jaxpr/gather | solution.py:59
  286.9 5.5 %gather_fusion = bf16[512,1024]{1,0:T(8,128)(2,1)S(1)} fusion(bf16[2048,1024]{1,0:T(8,128)(2,1)} %get-tuple-element.218, s32[1024]{0:T(1024)S(1)} %pad_clamp_fusion.4), kind=kCustom, calls=%fused_computation.1.clone.1 | custom fusion | bytes 2099200 | tf_op jit(solution)/shard_map/while/body/eval_jaxpr/gather | solution.py:60
  292.6 5.5 %gather_fusion.1 = bf16[512,1024]{1,0:T(8,128)(2,1)S(1)} fusion(bf16[2048,1024]{1,0:T(8,128)(2,1)} %get-tuple-element.218, s32[1024]{0:T(1024)S(1)} %pad_clamp_fusion.5), kind=kCustom, calls=%fused_computation.clone.1 | custom fusion | bytes 2099200 | tf_op jit(solution)/shard_map/while/body/eval_jaxpr/gather | solution.py:59
  300.7 5.5 %gather_fusion = bf16[512,1024]{1,0:T(8,128)(2,1)S(1)} fusion(bf16[2048,1024]{1,0:T(8,128)(2,1)} %get-tuple-element.218, s32[1024]{0:T(1024)S(1)} %pad_clamp_fusion.4), kind=kCustom, calls=%fused_computation.1.clone.1 | custom fusion | bytes 2099200 | tf_op jit(solution)/shard_map/while/body/eval_jaxpr/gather | solution.py:60
  306.4 5.5 %gather_fusion.1 = bf16[512,1024]{1,0:T(8,128)(2,1)S(1)} fusion(bf16[2048,1024]{1,0:T(8,128)(2,1)} %get-tuple-element.218, s32[1024]{0:T(1024)S(1)} %pad_clamp_fusion.5), kind=kCustom, calls=%fused_computation.clone.1 | custom fusion | bytes 2099200 | tf_op jit(solution)/shard_map/while/body/eval_jaxpr/gather | solution.py:59
  314.4 5.5 %gather_fusion = bf16[512,1024]{1,0:T(8,128)(2,1)S(1)} fusion(bf16[2048,1024]{1,0:T(8,128)(2,1)} %get-tuple-element.218, s32[1024]{0:T(1024)S(1)} %pad_clamp_fusion.4), kind=kCustom, calls=%fused_computation.1.clone.1 | custom fusion | bytes 2099200 | tf_op jit(solution)/shard_map/while/body/eval_jaxpr/gather | solution.py:60
  320.2 5.5 %gather_fusion.1 = bf16[512,1024]{1,0:T(8,128)(2,1)S(1)} fusion(bf16[2048,1024]{1,0:T(8,128)(2,1)} %get-tuple-element.218, s32[1024]{0:T(1024)S(1)} %pad_clamp_fusion.5), kind=kCustom, calls=%fused_computation.clone.1 | custom fusion | bytes 2099200 | tf_op jit(solution)/shard_map/while/body/eval_jaxpr/gather | solution.py:59
  328.2 5.5 %gather_fusion = bf16[512,1024]{1,0:T(8,128)(2,1)S(1)} fusion(bf16[2048,1024]{1,0:T(8,128)(2,1)} %get-tuple-element.218, s32[1024]{0:T(1024)S(1)} %pad_clamp_fusion.4), kind=kCustom, calls=%fused_computation.1.clone.1 | custom fusion | bytes 2099200 | tf_op jit(solution)/shard_map/while/body/eval_jaxpr/gather | solution.py:60
  333.9 5.5 %gather_fusion.1 = bf16[512,1024]{1,0:T(8,128)(2,1)S(1)} fusion(bf16[2048,1024]{1,0:T(8,128)(2,1)} %get-tuple-element.218, s32[1024]{0:T(1024)S(1)} %pad_clamp_fusion.5), kind=kCustom, calls=%fused_computation.clone.1 | custom fusion | bytes 2099200 | tf_op jit(solution)/shard_map/while/body/eval_jaxpr/gather | solution.py:59
  355.7 5.5 %gather_fusion = bf16[512,1024]{1,0:T(8,128)(2,1)S(1)} fusion(bf16[2048,1024]{1,0:T(8,128)(2,1)} %get-tuple-element.218, s32[1024]{0:T(1024)S(1)} %pad_clamp_fusion.4), kind=kCustom, calls=%fused_computation.1.clone.1 | custom fusion | bytes 2099200 | tf_op jit(solution)/shard_map/while/body/eval_jaxpr/gather | solution.py:60
  361.4 5.5 %gather_fusion.1 = bf16[512,1024]{1,0:T(8,128)(2,1)S(1)} fusion(bf16[2048,1024]{1,0:T(8,128)(2,1)} %get-tuple-element.218, s32[1024]{0:T(1024)S(1)} %pad_clamp_fusion.5), kind=kCustom, calls=%fused_computation.clone.1 | custom fusion | bytes 2099200 | tf_op jit(solution)/shard_map/while/body/eval_jaxpr/gather | solution.py:59
  369.5 5.5 %gather_fusion = bf16[512,1024]{1,0:T(8,128)(2,1)S(1)} fusion(bf16[2048,1024]{1,0:T(8,128)(2,1)} %get-tuple-element.218, s32[1024]{0:T(1024)S(1)} %pad_clamp_fusion.4), kind=kCustom, calls=%fused_computation.1.clone.1 | custom fusion | bytes 2099200 | tf_op jit(solution)/shard_map/while/body/eval_jaxpr/gather | solution.py:60
  (240 shorter events, 125.9 us)
Async XLA Ops:
  6.5 8.6 %copy-start.4 = (bf16[8,3,64]{2,0,1:T(8,128)(2,1)S(1)}, bf16[8,3,64]{2,0,1:T(8,128)(2,1)}, u32[]{:S(2)}) copy-start(bf16[8,3,64]{2,0,1:T(8,128)(2,1)} %param.10) | copy-start | bytes 9220
  6.5 8.6 %copy-start.2 = (bf16[8,1024]{1,0:T(8,128)(2,1)S(1)}, bf16[8,1024]{1,0:T(8,128)(2,1)}, u32[]{:S(2)}) copy-start(bf16[8,1024]{1,0:T(8,128)(2,1)} %param.11) | copy-start | bytes 49156
  6.5 8.7 %copy-start.3 = (s32[32,64]{1,0:T(8,128)S(1)}, s32[32,64]{1,0:T(8,128)}, u32[]{:S(2)}) copy-start(s32[32,64]{1,0:T(8,128)} %param.12) | copy-start | bytes 24580
  30.1 7.2 %copy-start.1 = (s32[2,8192]{1,0:T(2,128)S(1)}, s32[2,8192]{1,0:T(2,128)}, u32[]{:S(2)}) copy-start(s32[2,8192]{1,0:T(2,128)} %param.15) | copy-start | bytes 196612
  30.1 7.4 %copy-start.5 = (s32[64]{0:T(128)S(1)}, s32[64]{0:T(128)}, u32[]{:S(2)}) copy-start(s32[64]{0:T(128)} %param.14) | copy-start | bytes 772
  30.1 159.2 %copy-start.6 = (s32[64]{0:T(128)S(1)}, s32[64]{0:T(128)}, u32[]{:S(2)}) copy-start(s32[64]{0:T(128)} %param.13) | copy-start | bytes 772
  30.1 160.4 %all-to-all-start = ((bf16[32,64,1024]{2,1,0:T(8,128)(2,1)}), bf16[32,64,1024]{2,1,0:T(8,128)(2,1)}, u32[]{:S(2)}, u32[]{:S(2)}) async-start(bf16[32,64,1024]{2,1,0:T(8,128)(2,1)} %bitcast.58), calls=%async_computation | async-start | bytes 8388608 | tf_op jit(solution)/shard_map/all_to_all | solution.py:92
  36.6 152.7 %all-reduce.2.cloned.1.call-start = ((), (), s32[]{:S(2)}) async-start(), calls=%async_computation.1 | async-start | bytes 262144 | tf_op jit(solution)/shard_map/psum | solution.py:87
  202.0 1.0 copy-start
  215.8 1.0 copy-start
  229.6 1.0 copy-start
  243.3 1.0 copy-start
  257.1 1.0 copy-start
  270.8 1.0 copy-start
  284.6 1.0 copy-start
  298.4 1.0 copy-start
  312.1 1.0 copy-start
  325.9 1.0 copy-start
  339.7 1.0 copy-start
  353.4 1.0 copy-start
  367.2 1.0 copy-start
  380.9 1.0 copy-start
  394.7 1.0 copy-start
  408.5 1.0 copy-start
Sparse Core Ops, SparseCore 0:
  43.0 146.3 all-reduce.1
where the time goes:
time: 423 us; the launch traced here: 418 us
  local copies, waits for them, and re-layouts  191 us (45%)
  waiting for transfers between devices  149 us (35%)
  other arithmetic  33.9 us (8%)
  matrix products  22.1 us (5%)
  between operations  13.6 us (3%)
  starting transfers between devices  6.48 us (2%)
    psum x1, waiting for transfers between devices, shards(): power_sum = lax.psum(local_power, 'ev')  149 us
    gather x16, local copies, waits for them, and re-layouts, correlate_group(): second_spec = spectra[second_rows].astype(jnp.float32)  87.3 us
    gather x16, local copies, waits for them, and re-layouts, correlate_group(): first_spec = spectra[first_rows].astype(jnp.float32)  87.3 us
    another operation x18, other arithmetic  19.9 us
    dot_general x16, matrix products, correlate_group(): lagged = jnp.dot(cross_spec, lag_tab, preferred_element_type=jnp.float32)  19.7 us
    gather x1, local copies, waits for them, and re-layouts, shards(): own_rows[send_rows]  9.66 us
  transfers between devices with their start and end apart: 2, of which 1 were waited for; matrix products, arithmetic and copies ran while one was open for 1% of the time, Pallas kernels for 0%

commit v1 on v0

v1 whole, which is shorter than its diff:
```python
from functools import partial
import math

import jax
import jax.numpy as jnp
import numpy as np
from jax import lax
from jax.experimental import pallas as pl
from jax.experimental.pallas import tpu as pltpu
from jax.sharding import PartitionSpec as P

LAGS = 255
GROUP = 8
epsilon = 1e-06


def spectral_table(length):
    half_len = length // 2
    samples = np.arange(length, dtype=np.int32)[:, None]
    frequency = np.arange(half_len, dtype=np.int32)[None, :]
    angles = (samples * frequency % length).astype(np.float32) * np.float32(2.0 * math.pi / length)
    factor = np.float32(1.0 / math.sqrt(length))
    return jnp.asarray(
        np.concatenate([np.cos(angles) * factor, -np.sin(angles) * factor], axis=1), jnp.bfloat16
    )


def lag_table(length, lag_count):
    half_len = length // 2
    frequency = np.arange(half_len, dtype=np.int32)[:, None]
    shifts = np.arange(lag_count, dtype=np.int32)[None, :] - lag_count // 2
    angles = (frequency * shifts % length).astype(np.float32) * np.float32(2.0 * math.pi / length)
    factor = np.float32(1.0 / math.sqrt(half_len))
    return jnp.asarray(
        np.concatenate([np.cos(angles) * factor, -np.sin(angles) * factor], axis=0), jnp.bfloat16
    )


def exchange_kernel(
    n, events_total, win_ref, rot_ref, inv_ref, send_ref, table_ref,
    recv_ref, weight_ref,
    spectra, power, msg, part_out, part_in, w_in,
    send_sem, recv_sem, psend, precv, wsend, wrecv, local_sem,
):
    me = lax.axis_index("ev")
    grp = lax.axis_index("grp")
    mesh_id = pl.DeviceIdType.MESH
    ev_dev, comps, stations, length = win_ref.shape
    half = length // 2
    cap = recv_ref.shape[1]
    own = stations // n
    peers = range(1, n)

    barrier = pltpu.get_barrier_semaphore()

    @pl.loop(1, n)
    def _(s):
        pl.semaphore_signal(
            barrier, inc=1, device_id=(grp, lax.rem(me + s, n)), device_id_type=mesh_id
        )

    power[...] = jnp.zeros_like(power)
    diag = lax.broadcasted_iota(jnp.int32, (stations, stations), 0) == lax.broadcasted_iota(
        jnp.int32, (stations, stations), 1
    )
    inv_all = inv_ref[...].astype(jnp.float32)
    event_id = lax.broadcasted_iota(jnp.int32, (ev_dev, length), 0)

    @pl.loop(0, ev_dev)
    def _(e):
        rot = rot_ref[e].astype(jnp.float32)
        acc = None
        for c in range(comps):
            col = jnp.sum(
                jnp.where(diag, jnp.broadcast_to(rot[c : c + 1, :], diag.shape), 0.0),
                axis=1, keepdims=True,
            )
            term = col * win_ref[e, c].astype(jnp.float32)
            acc = term if acc is None else acc + term
        spec = jnp.dot(
            acc.astype(jnp.bfloat16), table_ref[...], preferred_element_type=jnp.float32
        )
        gain = jnp.sum(jnp.where(event_id == e, inv_all, 0.0), axis=0, keepdims=True)
        re, im = spec[:, :half], spec[:, half:]
        g_re, g_im = gain[:, :half], gain[:, half:]
        d_re = re * g_re - im * g_im
        d_im = re * g_im + im * g_re
        power[...] += d_re * d_re + d_im * d_im
        row = pl.multiple_of(e * stations, stations)
        spectra[pl.ds(row, stations), :half] = d_re.astype(jnp.bfloat16)
        spectra[pl.ds(row, stations), half:] = d_im.astype(jnp.bfloat16)

    pl.semaphore_wait(barrier, n - 1)

    for j in range(n):
        part_out[j] = power[j * own : (j + 1) * own, :]

    def part_copy(s):
        return pltpu.make_async_remote_copy(
            src_ref=part_out.at[lax.rem(me + s, n)], dst_ref=part_in.at[s],
            send_sem=psend.at[s], recv_sem=precv.at[s],
            device_id=(grp, lax.rem(me + s, n)), device_id_type=mesh_id,
        )

    @pl.loop(1, n)
    def _(s):
        part_copy(s).start()

    def msg_copy(s):
        target = lax.rem(me + s, n)
        return pltpu.make_async_remote_copy(
            src_ref=msg.at[target], dst_ref=recv_ref.at[me],
            send_sem=send_sem.at[s], recv_sem=recv_sem.at[s],
            device_id=(grp, target), device_id_type=mesh_id,
        )

    rows = ev_dev * stations
    row_id = lax.broadcasted_iota(jnp.int32, (rows, GROUP * cap), 0)

    @pl.loop(0, n // GROUP)
    def _(g):
        pick = (row_id == send_ref[pl.ds(g, 1), :]).astype(jnp.float32).astype(jnp.bfloat16)
        got = lax.dot_general(
            pick, spectra[...], (((0,), (0,)), ((), ())), preferred_element_type=jnp.float32
        )
        msg[pl.ds(pl.multiple_of(g * GROUP, GROUP), GROUP)] = got.astype(jnp.bfloat16).reshape(
            GROUP, cap, length
        )

    own_copy = pltpu.make_async_copy(msg.at[me], recv_ref.at[me], local_sem)
    own_copy.start()

    @pl.loop(1, n)
    def _(s):
        part_copy(s).wait_recv()

    total = part_out[me]
    for s in peers:
        total = total + part_in[s]
    w_own = 1.0 / (total / events_total + epsilon)
    w_in[0] = w_own

    def w_copy(s):
        return pltpu.make_async_remote_copy(
            src_ref=w_in.at[0], dst_ref=w_in.at[s],
            send_sem=wsend.at[s], recv_sem=wrecv.at[s],
            device_id=(grp, lax.rem(me + s, n)), device_id_type=mesh_id,
        )

    @pl.loop(1, n)
    def _(s):
        w_copy(s).start()

    @pl.loop(1, n)
    def _(s):
        msg_copy(s).start()

    @pl.loop(1, n)
    def _(s):
        w_copy(s).wait()

    for j in range(n):
        weight_ref[j * own : (j + 1) * own, :] = w_in[lax.rem(me - j + n, n)]

    own_copy.wait()

    @pl.loop(1, n)
    def _(s):
        part_copy(s).wait_send()
        msg_copy(s).wait()


def pair_kernel(
    tiles_step, tile_pairs, station_ref, count_ref, recv_ref, weight_ref, first_ref, second_ref,
    lag_ref, out_ref, rows_ref,
):
    step = pl.program_id(0)
    senders, per_chunk, length = recv_ref.shape
    half = length // 2
    sub = 8
    wide = recv_ref[...].astype(jnp.float32)
    for h in range(per_chunk // sub):
        rows_ref[h] = (
            wide[:, h * sub : (h + 1) * sub, :].reshape(senders * sub, length).astype(jnp.bfloat16)
        )
    live_id = lax.broadcasted_iota(jnp.int32, (tile_pairs, out_ref.shape[1]), 0)
    slot_id = lax.broadcasted_iota(jnp.int32, (senders * sub, tile_pairs), 0)
    slots = station_ref.shape[0]

    @pl.loop(0, tiles_step)
    def _(i):
        tile = step * tiles_step + i
        h = i // sub
        k = lax.rem(i, sub)

        def member(ref):
            place = (ref[pl.ds(i, 1), :] // slots) * sub + k
            pick = (slot_id == place).astype(jnp.float32).astype(jnp.bfloat16)
            return lax.dot_general(
                pick, rows_ref[h], (((0,), (0,)), ((), ())), preferred_element_type=jnp.float32
            )

        a, b = member(first_ref), member(second_ref)
        w = weight_ref[pl.ds(station_ref[tile], 1), :]
        a_re, a_im, b_re, b_im = a[:, :half], a[:, half:], b[:, :half], b[:, half:]
        cross = jnp.concatenate(
            [
                ((a_re * b_re + a_im * b_im) * w).astype(jnp.bfloat16),
                ((a_im * b_re - a_re * b_im) * w).astype(jnp.bfloat16),
            ],
            axis=1,
        )
        lagged = jnp.dot(cross, lag_ref[...], preferred_element_type=jnp.float32)
        row = pl.multiple_of(i * tile_pairs, tile_pairs)
        out_ref[pl.ds(row, tile_pairs), :] = jnp.where(live_id < count_ref[tile], lagged, 0.0)


def shards(windows, rotation, source_inverse, send_rows, tile_station, tile_count, pair_rows):
    ev_dev, comps, stations, length = windows.shape
    half = length // 2
    n = lax.axis_size("ev")
    cap = send_rows.shape[1]
    own = stations // n
    dma = pltpu.SemaphoreType.DMA
    vmem = pl.BlockSpec(memory_space=pltpu.VMEM)
    received, weight = pl.pallas_call(
        partial(exchange_kernel, n, ev_dev * n),
        out_shape=(
            jax.ShapeDtypeStruct((n, cap, length), jnp.bfloat16),
            jax.ShapeDtypeStruct((stations, half), jnp.float32),
        ),
        in_specs=[vmem] * 5,
        out_specs=(pl.BlockSpec(memory_space=pl.ANY), vmem),
        scratch_shapes=[
            pltpu.VMEM((ev_dev * stations, length), jnp.bfloat16),
            pltpu.VMEM((stations, half), jnp.float32),
            pltpu.VMEM((n, cap, length), jnp.bfloat16),
            pltpu.VMEM((n, own, half), jnp.float32),
            pltpu.VMEM((n, own, half), jnp.float32),
            pltpu.VMEM((n, own, half), jnp.float32),
            dma((n,)), dma((n,)), dma((n,)), dma((n,)), dma((n,)), dma((n,)), dma,
        ],
        compiler_params=pltpu.CompilerParams(
            collective_id=0, has_side_effects=True, vmem_limit_bytes=40 << 20
        ),
        name="exchange",
    )(
        windows, rotation, source_inverse, send_rows.reshape(n // GROUP, GROUP * cap),
        spectral_table(length),
    )

    tiles = tile_station.shape[0]
    tile_pairs = pair_rows.shape[1] // tiles
    senders = n * cap // tiles
    received = received.reshape(senders, tiles, length)
    step = 16
    members = pair_rows.reshape(2, tiles, tile_pairs)
    smem = pl.BlockSpec(memory_space=pltpu.SMEM)
    return pl.pallas_call(
        partial(pair_kernel, step, tile_pairs),
        grid=(tiles // step,),
        out_shape=jax.ShapeDtypeStruct((tiles * tile_pairs, LAGS), jnp.float32),
        in_specs=[
            smem,
            smem,
            pl.BlockSpec((senders, step, length), lambda i: (0, i, 0)),
            pl.BlockSpec((stations, half), lambda i: (0, 0)),
            pl.BlockSpec((None, step, tile_pairs), lambda i: (0, i, 0)),
            pl.BlockSpec((None, step, tile_pairs), lambda i: (1, i, 0)),
            pl.BlockSpec((length, LAGS), lambda i: (0, 0)),
        ],
        out_specs=pl.BlockSpec((step * tile_pairs, LAGS), lambda i: (i, 0)),
        scratch_shapes=[pltpu.VMEM((step // 8, senders * 8, length), jnp.bfloat16)],
        compiler_params=pltpu.CompilerParams(vmem_limit_bytes=48 << 20),
        name="pairs",
    )(tile_station, tile_count, received, weight, members, members, lag_table(length, LAGS))


def solution(mesh):
    in_specs = (
        P(("grp", "ev"), None, None, None),
        P(("grp", "ev"), None, None),
        P(("grp", "ev"), None),
        P(("grp", "ev"), None),
        P(("grp", "ev")),
        P(("grp", "ev")),
        P(None, ("grp", "ev")),
    )
    out_specs = P(("grp", "ev"), None)
    return jax.shard_map(shards, mesh=mesh, in_specs=in_specs, out_specs=out_specs, check_vma=False)
```

time: 423 us -> 171 us (0.40)
  the two profiles are of different devices: /device:TPU:7 before, /device:TPU:15 now
where the time goes in v1:
time: 171 us
  Pallas kernels  164 us (96%)
  local copies, waits for them, and re-layouts  6.57 us (4%)
    pallas_call x1, Pallas kernels, shards(): pl.pallas_call(partial(exchange_kernel, n, ev_dev * n), out_shape=(jax.Sh...  123 us
    pallas_call x1, Pallas kernels, shards(): pl.pallas_call(partial(pair_kernel, step, tile_pairs), grid=(tiles // ste...  41.2 us
    unnamed x14, local copies, waits for them, and re-layouts  5.77 us

profile of v1, /device:TPU:15, one launch (start us, length us, event | category | flops | bytes accessed | tf_op | source)
XLA Modules:
  0.0 170.8 jit_solution(776966156725663518)
XLA Ops:
  0.0 0.0 copy-start.5
  0.0 0.0 copy-start.4
  0.0 0.7 copy.10.rot_ref
  0.7 0.8 reshape.6.send_ref
  1.5 0.8 copy.13
  2.4 0.0 copy-start
  2.4 1.9 %copy-done = bf16[8,3,64,1024]{3,2,1,0:T(8,128)(2,1)S(1)} copy-done((bf16[8,3,64,1024]{3,2,1,0:T(8,128)(2,1)S(1)}, bf16[8,3,64,1024]{3,2,1,0:T(8,128)(2,1)}, u32[]{:S(2)}) %copy-start) | copy-done | bytes 3145752
  4.3 0.0 copy-start.1
  4.3 1.6 copy-done.1
  5.8 0.0 copy-start.3
  5.9 0.7 copy-done.3
  6.6 0.0 copy-start.2
  6.6 122.9 %exchange.1 = (bf16[32,64,1024]{2,1,0:T(8,128)(2,1)S(1)}, f32[64,512]{1,0:T(8,128)S(1)}) custom-call(bf16[8,3,64,1024]{3,2,1,0:T(8,128)(2,1)S(1)} %copy-done, bf16[8,3,64]{2,1,0:T(4,128)(2,1)S(1)} %copy.10.rot_ref, bf16[8,1024]{1,0:T(8,128)(2,1)S(1)} %copy-done.3, s32[4,512]{1,0:T(4,128)S(1)} %reshape.6.send_ref, bf16[1024,1024]{1,0:T(8,128)(2,1)S(1)} %copy-done.1), custom_call_target="tpu_custom_call" | custom-call | tf_op jit(solution)/shard_map/exchange/pallas_call | solution.py:226
  129.5 0.0 copy-done.5
  129.5 0.0 copy-done.4
  129.5 0.0 copy-done.2
  129.5 41.2 %pairs.1 = f32[8192,255]{1,0:T(8,128)} custom-call(s32[64]{0:T(128)S(1)} %copy-done.4, s32[64]{0:T(128)S(1)} %copy-done.5, bf16[32,64,1024]{2,1,0:T(8,128)(2,1)S(1)} %get-tuple-element.7.recv_ref, f32[64,512]{1,0:T(8,128)S(1)} %get-tuple-element.8.weight_ref, s32[2,64,128]{2,1,0:T(8,128)S(1)} %bitcast.4, s32[2,64,128]{2,1,0:T(8,128)S(1)} %bitcast.5, ...), custom_call_target="tpu_custom_call" | custom-call | tf_op jit(solution)/shard_map/pairs/pallas_call | solution.py:259
Async XLA Ops:
  0.0 129.5 %copy-start.5 = (s32[64]{0:T(128)S(1)}, s32[64]{0:T(128)}, u32[]{:S(2)}) copy-start(s32[64]{0:T(128)} %count_ref.1) | copy-start | bytes 772
  0.0 129.5 %copy-start.4 = (s32[64]{0:T(128)S(1)}, s32[64]{0:T(128)}, u32[]{:S(2)}) copy-start(s32[64]{0:T(128)} %station_ref.1) | copy-start | bytes 772
  2.4 1.9 %copy-start = (bf16[8,3,64,1024]{3,2,1,0:T(8,128)(2,1)S(1)}, bf16[8,3,64,1024]{3,2,1,0:T(8,128)(2,1)}, u32[]{:S(2)}) copy-start(bf16[8,3,64,1024]{3,2,1,0:T(8,128)(2,1)} %win_ref.1) | copy-start | bytes 9437188
  4.3 1.6 copy-start.1
  5.8 0.7 copy-start.3
  6.6 123.0 %copy-start.2 = (bf16[1024,255]{1,0:T(8,128)(2,1)S(1)}, bf16[1024,255]{1,0:T(8,128)(2,1)}, u32[]{:S(2)}) copy-start(bf16[1024,255]{1,0:T(8,128)(2,1)} %constant.5.clone.lag_ref) | copy-start | bytes 1566724

commit v2 on v1

--- a/solution.py
+++ b/solution.py
@@ -39,8 +39,8 @@
 def exchange_kernel(
     n, events_total, win_ref, rot_ref, inv_ref, send_ref, table_ref,
     recv_ref, weight_ref,
-    spectra, power, msg, part_out, part_in, w_in,
-    send_sem, recv_sem, psend, precv, wsend, wrecv, local_sem,
+    spectra, power, msg, part_out, part_in, w_in, far_spectra, far_send, far_msg,
+    send_sem, recv_sem, psend, precv, wsend, wrecv, fsend, frecv, rsend, isem, local_sem,
 ):
     me = lax.axis_index("ev")
     grp = lax.axis_index("grp")
@@ -49,7 +49,18 @@
     half = length // 2
     cap = recv_ref.shape[1]
     own = stations // n
-    peers = range(1, n)
+    near = n // 2
+    side = me // near
+    base = side * near
+    quarter = me // (n // 4)
+    inner = (quarter == 1) | (quarter == 2)
+    partner = lax.rem(me + n // 4 + side * near, n)
+
+    def remote(src, dst, ssem, rsem, target):
+        return pltpu.make_async_remote_copy(
+            src_ref=src, dst_ref=dst, send_sem=ssem, recv_sem=rsem,
+            device_id=(grp, target), device_id_type=mesh_id,
+        )
 
     barrier = pltpu.get_barrier_semaphore()
 
@@ -65,6 +76,18 @@
     )
     inv_all = inv_ref[...].astype(jnp.float32)
     event_id = lax.broadcasted_iota(jnp.int32, (ev_dev, length), 0)
+    pl.semaphore_wait(barrier, n - 1)
+
+    def index_copy():
+        return remote(send_ref, far_send, isem.at[0], isem.at[1], partner)
+
+    def far_copy(e):
+        row = pl.ds(pl.multiple_of(e * stations, stations), stations)
+        return remote(spectra.at[row], far_spectra.at[row], fsend.at[e], frecv.at[e], partner)
+
+    @pl.when(inner)
+    def _():
+        index_copy().start()
 
     @pl.loop(0, ev_dev)
     def _(e):
@@ -90,70 +113,113 @@
         spectra[pl.ds(row, stations), :half] = d_re.astype(jnp.bfloat16)
         spectra[pl.ds(row, stations), half:] = d_im.astype(jnp.bfloat16)
 
-    pl.semaphore_wait(barrier, n - 1)
+        @pl.when(inner)
+        def _():
+            far_copy(e).start()
 
     for j in range(n):
         part_out[j] = power[j * own : (j + 1) * own, :]
 
     def part_copy(s):
-        return pltpu.make_async_remote_copy(
-            src_ref=part_out.at[lax.rem(me + s, n)], dst_ref=part_in.at[s],
-            send_sem=psend.at[s], recv_sem=precv.at[s],
-            device_id=(grp, lax.rem(me + s, n)), device_id_type=mesh_id,
-        )
+        target = lax.rem(me + s, n)
+        return remote(part_out.at[target], part_in.at[s], psend.at[s], precv.at[s], target)
 
     @pl.loop(1, n)
     def _(s):
         part_copy(s).start()
-
-    def msg_copy(s):
-        target = lax.rem(me + s, n)
-        return pltpu.make_async_remote_copy(
-            src_ref=msg.at[target], dst_ref=recv_ref.at[me],
-            send_sem=send_sem.at[s], recv_sem=recv_sem.at[s],
-            device_id=(grp, target), device_id_type=mesh_id,
-        )
 
     rows = ev_dev * stations
     row_id = lax.broadcasted_iota(jnp.int32, (rows, GROUP * cap), 0)
 
-    @pl.loop(0, n // GROUP)
-    def _(g):
-        pick = (row_id == send_ref[pl.ds(g, 1), :]).astype(jnp.float32).astype(jnp.bfloat16)
+    def gather(index_ref, from_ref, to_ref, g, place):
+        pick = (row_id == index_ref[pl.ds(g, 1), :]).astype(jnp.float32).astype(jnp.bfloat16)
         got = lax.dot_general(
-            pick, spectra[...], (((0,), (0,)), ((), ())), preferred_element_type=jnp.float32
-        )
-        msg[pl.ds(pl.multiple_of(g * GROUP, GROUP), GROUP)] = got.astype(jnp.bfloat16).reshape(
+            pick, from_ref[...], (((0,), (0,)), ((), ())), preferred_element_type=jnp.float32
+        )
+        to_ref[pl.ds(pl.multiple_of(place, GROUP), GROUP)] = got.astype(jnp.bfloat16).reshape(
             GROUP, cap, length
         )
 
-    own_copy = pltpu.make_async_copy(msg.at[me], recv_ref.at[me], local_sem)
+    def msg_copy(target):
+        return remote(
+            msg.at[target], recv_ref.at[me], send_sem.at[target], recv_sem.at[me], target
+        )
+
+    def near_target(s):
+        return base + lax.rem(me - base + s, near)
+
+    def far_target(s):
+        return near - base + lax.rem(me - base + s, near)
+
+    side_groups = near // GROUP
+
+    @pl.loop(0, side_groups)
+    def _(i):
+        g = side * side_groups + i
+        gather(send_ref, spectra, msg, g, g * GROUP)
+
+    own_copy = pltpu.make_async_copy(msg.at[me], recv_ref.at[me], local_sem.at[0])
     own_copy.start()
 
+    @pl.loop(1, near)
+    def _(s):
+        msg_copy(near_target(s)).start()
+
+    @pl.when(jnp.logical_not(inner))
+    def _():
+        @pl.loop(0, side_groups)
+        def _(i):
+            g = (1 - side) * side_groups + i
+            gather(send_ref, spectra, msg, g, g * GROUP)
+
+        @pl.loop(0, near)
+        def _(s):
+            msg_copy(far_target(s)).start()
+
     @pl.loop(1, n)
     def _(s):
         part_copy(s).wait_recv()
 
     total = part_out[me]
-    for s in peers:
+    for s in range(1, n):
         total = total + part_in[s]
-    w_own = 1.0 / (total / events_total + epsilon)
-    w_in[0] = w_own
+    w_in[0] = 1.0 / (total / events_total + epsilon)
 
     def w_copy(s):
-        return pltpu.make_async_remote_copy(
-            src_ref=w_in.at[0], dst_ref=w_in.at[s],
-            send_sem=wsend.at[s], recv_sem=wrecv.at[s],
-            device_id=(grp, lax.rem(me + s, n)), device_id_type=mesh_id,
-        )
+        return remote(w_in.at[0], w_in.at[s], wsend.at[s], wrecv.at[s], lax.rem(me + s, n))
 
     @pl.loop(1, n)
     def _(s):
         w_copy(s).start()
 
-    @pl.loop(1, n)
-    def _(s):
-        msg_copy(s).start()
+    def relay_copy(target):
+        return remote(
+            far_msg.at[target - base], recv_ref.at[partner], rsend.at[target - base],
+            recv_sem.at[partner], target,
+        )
+
+    def partner_copy():
+        return pltpu.make_async_copy(
+            far_msg.at[me - base], recv_ref.at[partner], local_sem.at[1]
+        )
+
+    @pl.when(inner)
+    def _():
+        index_copy().wait()
+
+        @pl.loop(0, ev_dev)
+        def _(e):
+            far_copy(e).wait()
+
+        @pl.loop(0, side_groups)
+        def _(i):
+            gather(far_send, far_spectra, far_msg, side * side_groups + i, i * GROUP)
+
+        partner_copy().start()
+
+        @pl.loop(1, near)
+        def _(s):
+            relay_copy(near_target(s)).start()
 
     @pl.loop(1, n)
     def _(s):
@@ -167,52 +233,101 @@
     @pl.loop(1, n)
     def _(s):
         part_copy(s).wait_send()
-        msg_copy(s).wait()
+
+    def arrived(source):
+        remote(
+            msg.at[source], recv_ref.at[source], send_sem.at[source], recv_sem.at[source], source
+        ).wait_recv()
+
+    @pl.loop(1, near)
+    def _(s):
+        msg_copy(near_target(s)).wait_send()
+        arrived(near_target(s))
+
+    @pl.when(jnp.logical_not(inner))
+    def _():
+        @pl.loop(0, near)
+        def _(s):
+            msg_copy(far_target(s)).wait_send()
+            arrived(far_target(s))
+
+    @pl.when(inner)
+    def _():
+        partner_copy().wait()
+
+        @pl.loop(0, near)
+        def _(s):
+            source = far_target(s)
+
+            @pl.when(source != partner)
+            def _():
+                arrived(source)
+
+        @pl.loop(1, near)
+        def _(s):
+            relay_copy(near_target(s)).wait_send()
 
 
 def pair_kernel(
-    tiles_step, tile_pairs, station_ref, count_ref, recv_ref, weight_ref, first_ref, second_ref,
-    lag_ref, out_ref, rows_ref,
+    batch, tile_pairs, station_ref, count_ref, recv_ref, weight_ref, first_ref, second_ref,
+    lag_ref, out_ref, rows_ref, cross_ref,
 ):
-    step = pl.program_id(0)
-    senders, per_chunk, length = recv_ref.shape
+    senders, per_step, length = recv_ref.shape
+    first_tile = pl.program_id(0) * per_step
     half = length // 2
     sub = 8
+    width = half // 2
+    slots = station_ref.shape[0]
     wide = recv_ref[...].astype(jnp.float32)
-    for h in range(per_chunk // sub):
+    for h in range(per_step // sub):
         rows_ref[h] = (
             wide[:, h * sub : (h + 1) * sub, :].reshape(senders * sub, length).astype(jnp.bfloat16)
         )
     live_id = lax.broadcasted_iota(jnp.int32, (tile_pairs, out_ref.shape[1]), 0)
-    slot_id = lax.broadcasted_iota(jnp.int32, (senders * sub, tile_pairs), 0)
-    slots = station_ref.shape[0]
-
-    @pl.loop(0, tiles_step)
-    def _(i):
-        tile = step * tiles_step + i
-        h = i // sub
-        k = lax.rem(i, sub)
-
-        def member(ref):
-            place = (ref[pl.ds(i, 1), :] // slots) * sub + k
-            pick = (slot_id == place).astype(jnp.float32).astype(jnp.bfloat16)
-            return lax.dot_general(
-                pick, rows_ref[h], (((0,), (0,)), ((), ())), preferred_element_type=jnp.float32
+    lane = lax.broadcasted_iota(jnp.int32, (tile_pairs, senders * sub), 1)
+
+    def places(ref):
+        r = ref[...]
+        k = lax.rem(lax.broadcasted_iota(jnp.int32, r.shape, 0), sub)
+        return jnp.transpose((r // slots) * sub + k)
+
+    def pick(place, t0):
+        return jnp.concatenate(
+            [
+                (lane == place[:, t : t + 1]).astype(jnp.float32).astype(jnp.bfloat16)
+                for t in range(t0, t0 + batch)
+            ],
+            axis=0,
+        )
+
+    first, second = places(first_ref), places(second_ref)
+    for t0 in range(0, per_step, batch):
+        h = t0 // sub
+        pick_a, pick_b = pick(first, t0), pick(second, t0)
+        for c in range(0, half, width):
+
+            def member(picked, at):
+                return jnp.dot(
+                    picked, rows_ref[h, :, at : at + width], preferred_element_type=jnp.float32
+                )
+
+            a_re, a_im = member(pick_a, c), member(pick_a, half + c)
+            b_re, b_im = member(pick_b, c), member(pick_b, half + c)
+            re = a_re * b_re + a_im * b_im
+            im = a_im * b_re - a_re * b_im
+            for j in range(batch):
+                station = station_ref[first_tile + t0 + j]
+                w = weight_ref[pl.ds(station, 1), c : c + width]
+                at = slice(j * tile_pairs, (j + 1) * tile_pairs)
+                cross_ref[at, c : c + width] = (re[at] * w).astype(jnp.bfloat16)
+                cross_ref[at, half + c : half + c + width] = (im[at] * w).astype(jnp.bfloat16)
+        lagged = jnp.dot(cross_ref[...], lag_ref[...], preferred_element_type=jnp.float32)
+        for j in range(batch):
+            at = (t0 + j) * tile_pairs
+            out_ref[at : at + tile_pairs, :] = jnp.where(
+                live_id < count_ref[first_tile + t0 + j],
+                lagged[j * tile_pairs : (j + 1) * tile_pairs], 0.0,
             )
-
-        a, b = member(first_ref), member(second_ref)
-        w = weight_ref[pl.ds(station_ref[tile], 1), :]
-        a_re, a_im, b_re, b_im = a[:, :half], a[:, half:], b[:, :half], b[:, half:]
-        cross = jnp.concatenate(
-            [
-                ((a_re * b_re + a_im * b_im) * w).astype(jnp.bfloat16),
-                ((a_im * b_re - a_re * b_im) * w).astype(jnp.bfloat16),
-            ],
-            axis=1,
-        )
-        lagged = jnp.dot(cross, lag_ref[...], preferred_element_type=jnp.float32)
-        row = pl.multiple_of(i * tile_pairs, tile_pairs)
-        out_ref[pl.ds(row, tile_pairs), :] = jnp.where(live_id < count_ref[tile], lagged, 0.0)
 
 
 def shards(windows, rotation, source_inverse, send_rows, tile_station, tile_count, pair_rows):
@@ -238,7 +353,11 @@
             pltpu.VMEM((n, own, half), jnp.float32),
             pltpu.VMEM((n, own, half), jnp.float32),
             pltpu.VMEM((n, own, half), jnp.float32),
-            dma((n,)), dma((n,)), dma((n,)), dma((n,)), dma((n,)), dma((n,)), dma,
+            pltpu.VMEM((ev_dev * stations, length), jnp.bfloat16),
+            pltpu.VMEM((n // GROUP, GROUP * cap), jnp.int32),
+            pltpu.VMEM((n // 2, cap, length), jnp.bfloat16),
+            dma((n,)), dma((n,)), dma((n,)), dma((n,)), dma((n,)), dma((n,)),
+            dma((ev_dev,)), dma((ev_dev,)), dma((n // 2,)), dma((2,)), dma((2,)),
         ],
         compiler_params=pltpu.CompilerParams(
             collective_id=0, has_side_effects=True, vmem_limit_bytes=40 << 20
@@ -253,11 +372,11 @@
     tile_pairs = pair_rows.shape[1] // tiles
     senders = n * cap // tiles
     received = received.reshape(senders, tiles, length)
-    step = 16
+    step, batch = 16, 4
     members = pair_rows.reshape(2, tiles, tile_pairs)
     smem = pl.BlockSpec(memory_space=pltpu.SMEM)
     return pl.pallas_call(
-        partial(pair_kernel, step, tile_pairs),
+        partial(pair_kernel, batch, tile_pairs),
         grid=(tiles // step,),
         out_shape=jax.ShapeDtypeStruct((tiles * tile_pairs, LAGS), jnp.float32),
         in_specs=[
@@ -270,7 +389,10 @@
             pl.BlockSpec((length, LAGS), lambda i: (0, 0)),
         ],
         out_specs=pl.BlockSpec((step * tile_pairs, LAGS), lambda i: (i, 0)),
-        scratch_shapes=[pltpu.VMEM((step // 8, senders * 8, length), jnp.bfloat16)],
+        scratch_shapes=[
+            pltpu.VMEM((step // 8, senders * 8, length), jnp.bfloat16),
+            pltpu.VMEM((batch * tile_pairs, length), jnp.bfloat16),
+        ],
         compiler_params=pltpu.CompilerParams(vmem_limit_bytes=48 << 20),
         name="pairs",
     )(tile_station, tile_count, received, weight, members, members, lag_table(length, LAGS))

time: 171 us -> 126 us (0.74)
  the two profiles are of different devices: /device:TPU:15 before, /device:TPU:7 now
where the time goes in v2:
time: 126 us
  Pallas kernels  119 us (94%)
  local copies, waits for them, and re-layouts  6.57 us (5%)
    pallas_call x1, Pallas kernels, shards(): pl.pallas_call(partial(exchange_kernel, n, ev_dev * n), out_shape=(jax.Sh...  99.8 us
    pallas_call x1, Pallas kernels, shards(): pl.pallas_call(partial(pair_kernel, batch, tile_pairs), grid=(tiles // st...  19.5 us
    unnamed x14, local copies, waits for them, and re-layouts  5.77 us

profile of v2, /device:TPU:7, one launch (start us, length us, event | category | flops | bytes accessed | tf_op | source)
XLA Modules:
  0.0 126.0 jit_solution(17234559572439670148)
XLA Ops:
  0.0 0.0 copy-start.5
  0.0 0.0 copy-start.4
  0.0 0.7 copy.10.rot_ref
  0.7 0.8 reshape.6.send_ref
  1.5 0.8 copy.13
  2.4 0.0 copy-start
  2.4 1.9 %copy-done = bf16[8,3,64,1024]{3,2,1,0:T(8,128)(2,1)S(1)} copy-done((bf16[8,3,64,1024]{3,2,1,0:T(8,128)(2,1)S(1)}, bf16[8,3,64,1024]{3,2,1,0:T(8,128)(2,1)}, u32[]{:S(2)}) %copy-start) | copy-done | bytes 3145752
  4.3 0.0 copy-start.1
  4.3 1.6 %copy-done.1 = bf16[1024,1024]{1,0:T(8,128)(2,1)S(1)} copy-done((bf16[1024,1024]{1,0:T(8,128)(2,1)S(1)}, bf16[1024,1024]{1,0:T(8,128)(2,1)}, u32[]{:S(2)}) %copy-start.1) | copy-done | bytes 2097176
  5.8 0.0 copy-start.3
  5.9 0.7 copy-done.3
  6.6 0.0 copy-start.2
  6.6 99.8 %exchange.1 = (bf16[32,64,1024]{2,1,0:T(8,128)(2,1)S(1)}, f32[64,512]{1,0:T(8,128)S(1)}) custom-call(bf16[8,3,64,1024]{3,2,1,0:T(8,128)(2,1)S(1)} %copy-done, bf16[8,3,64]{2,1,0:T(4,128)(2,1)S(1)} %copy.10.rot_ref, bf16[8,1024]{1,0:T(8,128)(2,1)S(1)} %copy-done.3, s32[4,512]{1,0:T(4,128)S(1)} %reshape.6.send_ref, bf16[1024,1024]{1,0:T(8,128)(2,1)S(1)} %copy-done.1), custom_call_target="tpu_custom_call" | custom-call | tf_op jit(solution)/shard_map/exchange/pallas_call | solution.py:341
  106.4 0.0 copy-done.5
  106.4 0.0 copy-done.4
  106.4 0.0 copy-done.2
  106.4 19.5 %pairs.1 = f32[8192,255]{1,0:T(8,128)} custom-call(s32[64]{0:T(128)S(1)} %copy-done.4, s32[64]{0:T(128)S(1)} %copy-done.5, bf16[32,64,1024]{2,1,0:T(8,128)(2,1)S(1)} %get-tuple-element.7.recv_ref, f32[64,512]{1,0:T(8,128)S(1)} %get-tuple-element.8.weight_ref, s32[2,64,128]{2,1,0:T(8,128)S(1)} %bitcast.4, s32[2,64,128]{2,1,0:T(8,128)S(1)} %bitcast.5, ...), custom_call_target="tpu_custom_call" | custom-call | tf_op jit(solution)/shard_map/pairs/pallas_call | solution.py:378
Async XLA Ops:
  0.0 106.4 %copy-start.5 = (s32[64]{0:T(128)S(1)}, s32[64]{0:T(128)}, u32[]{:S(2)}) copy-start(s32[64]{0:T(128)} %count_ref.1) | copy-start | bytes 772
  0.0 106.4 %copy-start.4 = (s32[64]{0:T(128)S(1)}, s32[64]{0:T(128)}, u32[]{:S(2)}) copy-start(s32[64]{0:T(128)} %station_ref.1) | copy-start | bytes 772
  2.4 1.9 %copy-start = (bf16[8,3,64,1024]{3,2,1,0:T(8,128)(2,1)S(1)}, bf16[8,3,64,1024]{3,2,1,0:T(8,128)(2,1)}, u32[]{:S(2)}) copy-start(bf16[8,3,64,1024]{3,2,1,0:T(8,128)(2,1)} %win_ref.1) | copy-start | bytes 9437188
  4.3 1.6 %copy-start.1 = (bf16[1024,1024]{1,0:T(8,128)(2,1)S(1)}, bf16[1024,1024]{1,0:T(8,128)(2,1)}, u32[]{:S(2)}) copy-start(bf16[1024,1024]{1,0:T(8,128)(2,1)} %constant.4.clone.table_ref) | copy-start | bytes 6291460
  5.8 0.7 copy-start.3
  6.6 99.9 %copy-start.2 = (bf16[1024,255]{1,0:T(8,128)(2,1)S(1)}, bf16[1024,255]{1,0:T(8,128)(2,1)}, u32[]{:S(2)}) copy-start(bf16[1024,255]{1,0:T(8,128)(2,1)} %constant.5.clone.lag_ref) | copy-start | bytes 1566724

commit v3 on v2

--- a/solution.py
+++ b/solution.py
@@ -37,15 +37,16 @@
 
 
 def exchange_kernel(
-    n, events_total, win_ref, rot_ref, inv_ref, send_ref, table_ref,
+    n, events_total, win_hbm, rot_ref, inv_ref, send_ref, table_hbm,
     recv_ref, weight_ref,
     spectra, power, msg, part_out, part_in, w_in, far_spectra, far_send, far_msg,
-    send_sem, recv_sem, psend, precv, wsend, wrecv, fsend, frecv, rsend, isem, local_sem,
+    win_ref, table_ref,
+    send_sem, recv_sem, psend, precv, wsend, wrecv, fsend, frecv, rsend, isem, local_sem, load_sem,
 ):
     me = lax.axis_index("ev")
     grp = lax.axis_index("grp")
     mesh_id = pl.DeviceIdType.MESH
-    ev_dev, comps, stations, length = win_ref.shape
+    ev_dev, comps, stations, length = win_hbm.shape
     half = length // 2
     cap = recv_ref.shape[1]
     own = stations // n
@@ -70,6 +71,17 @@
             barrier, inc=1, device_id=(grp, lax.rem(me + s, n)), device_id_type=mesh_id
         )
 
+    def win_copy(e):
+        return pltpu.make_async_copy(win_hbm.at[e], win_ref.at[e], load_sem.at[e])
+
+    table_copy = pltpu.make_async_copy(table_hbm, table_ref, load_sem.at[ev_dev])
+    win_copy(0).start()
+    table_copy.start()
+
+    @pl.loop(1, ev_dev)
+    def _(e):
+        win_copy(e).start()
+
     power[...] = jnp.zeros_like(power)
     diag = lax.broadcasted_iota(jnp.int32, (stations, stations), 0) == lax.broadcasted_iota(
         jnp.int32, (stations, stations), 1
@@ -89,8 +101,11 @@
     def _():
         index_copy().start()
 
+    table_copy.wait()
+
     @pl.loop(0, ev_dev)
     def _(e):
+        win_copy(e).wait()
         rot = rot_ref[e].astype(jnp.float32)
         acc = None
         for c in range(comps):
@@ -132,7 +147,10 @@
     row_id = lax.broadcasted_iota(jnp.int32, (rows, GROUP * cap), 0)
 
     def gather(index_ref, from_ref, to_ref, g, place):
-        pick = (row_id == index_ref[pl.ds(g, 1), :]).astype(jnp.float32).astype(jnp.bfloat16)
+        wanted = jnp.concatenate(
+            [index_ref[pl.ds(g * GROUP + r, 1), :] for r in range(GROUP)], axis=1
+        )
+        pick = (row_id == wanted).astype(jnp.float32).astype(jnp.bfloat16)
         got = lax.dot_general(
             pick, from_ref[...], (((0,), (0,)), ((), ())), preferred_element_type=jnp.float32
         )
@@ -269,7 +287,7 @@
 
 
 def pair_kernel(
-    batch, tile_pairs, station_ref, count_ref, recv_ref, weight_ref, first_ref, second_ref,
+    batch, tile_pairs, station_ref, count_ref, recv_ref, weight_ref, member_ref,
     lag_ref, out_ref, rows_ref, cross_ref,
 ):
     senders, per_step, length = recv_ref.shape
@@ -286,8 +304,14 @@
     live_id = lax.broadcasted_iota(jnp.int32, (tile_pairs, out_ref.shape[1]), 0)
     lane = lax.broadcasted_iota(jnp.int32, (tile_pairs, senders * sub), 1)
 
-    def places(ref):
-        r = ref[...]
+    def places(m):
+        r = jnp.concatenate(
+            [
+                member_ref[m : m + 1, t * tile_pairs : (t + 1) * tile_pairs]
+                for t in range(per_step)
+            ],
+            axis=0,
+        )
         k = lax.rem(lax.broadcasted_iota(jnp.int32, r.shape, 0), sub)
         return jnp.transpose((r // slots) * sub + k)
 
@@ -300,7 +324,7 @@
             axis=0,
         )
 
-    first, second = places(first_ref), places(second_ref)
+    first, second = places(0), places(1)
     for t0 in range(0, per_step, batch):
         h = t0 // sub
         pick_a, pick_b = pick(first, t0), pick(second, t0)
@@ -338,13 +362,14 @@
     own = stations // n
     dma = pltpu.SemaphoreType.DMA
     vmem = pl.BlockSpec(memory_space=pltpu.VMEM)
+    hbm = pl.BlockSpec(memory_space=pltpu.HBM)
     received, weight = pl.pallas_call(
         partial(exchange_kernel, n, ev_dev * n),
         out_shape=(
             jax.ShapeDtypeStruct((n, cap, length), jnp.bfloat16),
             jax.ShapeDtypeStruct((stations, half), jnp.float32),
         ),
-        in_specs=[vmem] * 5,
+        in_specs=[hbm, vmem, vmem, vmem, hbm],
         out_specs=(pl.BlockSpec(memory_space=pl.ANY), vmem),
         scratch_shapes=[
             pltpu.VMEM((ev_dev * stations, length), jnp.bfloat16),
@@ -354,17 +379,19 @@
             pltpu.VMEM((n, own, half), jnp.float32),
             pltpu.VMEM((n, own, half), jnp.float32),
             pltpu.VMEM((ev_dev * stations, length), jnp.bfloat16),
-            pltpu.VMEM((n // GROUP, GROUP * cap), jnp.int32),
+            pltpu.VMEM((n, cap), jnp.int32),
             pltpu.VMEM((n // 2, cap, length), jnp.bfloat16),
+            pltpu.VMEM((ev_dev, comps, stations, length), jnp.bfloat16),
+            pltpu.VMEM((length, length), jnp.bfloat16),
             dma((n,)), dma((n,)), dma((n,)), dma((n,)), dma((n,)), dma((n,)),
-            dma((ev_dev,)), dma((ev_dev,)), dma((n // 2,)), dma((2,)), dma((2,)),
+            dma((ev_dev,)), dma((ev_dev,)), dma((n // 2,)), dma((2,)), dma((2,)), dma((ev_dev + 1,)),
         ],
         compiler_params=pltpu.CompilerParams(
             collective_id=0, has_side_effects=True, vmem_limit_bytes=40 << 20
         ),
         name="exchange",
     )(
-        windows, rotation, source_inverse, send_rows.reshape(n // GROUP, GROUP * cap),
+        windows, rotation, source_inverse, send_rows,
         spectral_table(length),
     )
 
@@ -373,7 +400,6 @@
     senders = n * cap // tiles
     received = received.reshape(senders, tiles, length)
     step, batch = 16, 4
-    members = pair_rows.reshape(2, tiles, tile_pairs)
     smem = pl.BlockSpec(memory_space=pltpu.SMEM)
     return pl.pallas_call(
         partial(pair_kernel, batch, tile_pairs),
@@ -384,8 +410,7 @@
             smem,
             pl.BlockSpec((senders, step, length), lambda i: (0, i, 0)),
             pl.BlockSpec((stations, half), lambda i: (0, 0)),
-            pl.BlockSpec((None, step, tile_pairs), lambda i: (0, i, 0)),
-            pl.BlockSpec((None, step, tile_pairs), lambda i: (1, i, 0)),
+            pl.BlockSpec((2, step * tile_pairs), lambda i: (0, i)),
             pl.BlockSpec((length, LAGS), lambda i: (0, 0)),
         ],
         out_specs=pl.BlockSpec((step * tile_pairs, LAGS), lambda i: (i, 0)),
@@ -395,7 +420,7 @@
         ],
         compiler_params=pltpu.CompilerParams(vmem_limit_bytes=48 << 20),
         name="pairs",
-    )(tile_station, tile_count, received, weight, members, members, lag_table(length, LAGS))
+    )(tile_station, tile_count, received, weight, pair_rows, lag_table(length, LAGS))
 
 
 def solution(mesh):

time: 126 us -> 125 us (level)
    unnamed x14 -> x17, local copies, waits for them, and re-layouts: 5.77 us -> 5.65 us
where the time goes in v3:
time: 125 us
  Pallas kernels  119 us (95%)
  local copies, waits for them, and re-layouts  5.65 us (5%)
    pallas_call x1, Pallas kernels, shards(): pl.pallas_call(partial(exchange_kernel, n, ev_dev * n), out_shape=(jax.Sh...  99.7 us
    pallas_call x1, Pallas kernels, shards(): pl.pallas_call(partial(pair_kernel, batch, tile_pairs), grid=(tiles // st...  19.6 us
    unnamed x17, local copies, waits for them, and re-layouts  5.65 us

profile of v3, /device:TPU:7, one launch (start us, length us, event | category | flops | bytes accessed | tf_op | source)
XLA Modules:
  0.0 125.0 jit_solution(8807732005179708147)
XLA Ops:
  0.0 0.0 copy-start.7
  0.0 0.0 copy-start.6
  0.0 0.7 copy.10.rot_ref
  0.7 0.0 copy-start
  0.7 1.9 %copy-done = bf16[8,3,64,1024]{3,2,1,0:T(8,128)(2,1)S(1)} copy-done((bf16[8,3,64,1024]{3,2,1,0:T(8,128)(2,1)S(1)}, bf16[8,3,64,1024]{3,2,1,0:T(8,128)(2,1)}, u32[]{:S(2)}) %copy-start) | copy-done | bytes 3145752
  2.6 0.0 copy-start.1
  2.6 1.6 %copy-done.1 = bf16[1024,1024]{1,0:T(8,128)(2,1)S(1)} copy-done((bf16[1024,1024]{1,0:T(8,128)(2,1)S(1)}, bf16[1024,1024]{1,0:T(8,128)(2,1)}, u32[]{:S(2)}) %copy-start.1) | copy-done | bytes 2097176
  4.2 0.0 copy-start.4
  4.2 0.7 copy-done.4
  4.9 0.0 copy-start.5
  4.9 0.7 copy-done.5
  5.6 0.0 copy-start.2
  5.6 0.0 copy-start.3
  5.6 99.7 %exchange.1 = (bf16[32,64,1024]{2,1,0:T(8,128)(2,1)S(1)}, f32[64,512]{1,0:T(8,128)S(1)}) custom-call(bf16[8,3,64,1024]{3,2,1,0:T(8,128)(2,1)S(1)} %copy-done, bf16[8,3,64]{2,1,0:T(4,128)(2,1)S(1)} %copy.10.rot_ref, bf16[8,1024]{1,0:T(8,128)(2,1)S(1)} %copy-done.4, s32[32,64]{1,0:T(8,128)S(1)} %copy-done.5, bf16[1024,1024]{1,0:T(8,128)(2,1)S(1)} %copy-done.1), custom_call_target="tpu_custom_call" | custom-call | tf_op jit(solution)/shard_map/exchange/pallas_call | solution.py:366
  105.3 0.0 copy-done.7
  105.3 0.0 copy-done.6
  105.3 0.0 copy-done.2
  105.3 0.0 copy-done.3
  105.4 19.6 %pairs.1 = f32[8192,255]{1,0:T(8,128)} custom-call(s32[64]{0:T(128)S(1)} %copy-done.6, s32[64]{0:T(128)S(1)} %copy-done.7, bf16[32,64,1024]{2,1,0:T(8,128)(2,1)S(1)} %get-tuple-element.7.recv_ref, f32[64,512]{1,0:T(8,128)S(1)} %get-tuple-element.8.weight_ref, s32[2,8192]{1,0:T(2,128)S(1)} %copy-done.3, bf16[1024,255]{1,0:T(8,128)(2,1)S(1)} %copy-done.2), custom_call_target="tpu_custom_call" | custom-call | tf_op jit(solution)/shard_map/pairs/pallas_call | solution.py:404
Async XLA Ops:
  0.0 105.3 %copy-start.7 = (s32[64]{0:T(128)S(1)}, s32[64]{0:T(128)}, u32[]{:S(2)}) copy-start(s32[64]{0:T(128)} %count_ref.1) | copy-start | bytes 772
  0.0 105.3 %copy-start.6 = (s32[64]{0:T(128)S(1)}, s32[64]{0:T(128)}, u32[]{:S(2)}) copy-start(s32[64]{0:T(128)} %station_ref.1) | copy-start | bytes 772
  0.7 1.9 %copy-start = (bf16[8,3,64,1024]{3,2,1,0:T(8,128)(2,1)S(1)}, bf16[8,3,64,1024]{3,2,1,0:T(8,128)(2,1)}, u32[]{:S(2)}) copy-start(bf16[8,3,64,1024]{3,2,1,0:T(8,128)(2,1)} %win_hbm.1) | copy-start | bytes 9437188
  2.6 1.6 %copy-start.1 = (bf16[1024,1024]{1,0:T(8,128)(2,1)S(1)}, bf16[1024,1024]{1,0:T(8,128)(2,1)}, u32[]{:S(2)}) copy-start(bf16[1024,1024]{1,0:T(8,128)(2,1)} %constant.4.clone.table_hbm) | copy-start | bytes 6291460
  4.2 0.7 copy-start.4
  4.9 0.7 copy-start.5
  5.6 99.7 %copy-start.2 = (bf16[1024,255]{1,0:T(8,128)(2,1)S(1)}, bf16[1024,255]{1,0:T(8,128)(2,1)}, u32[]{:S(2)}) copy-start(bf16[1024,255]{1,0:T(8,128)(2,1)} %constant.5.clone.lag_ref) | copy-start | bytes 1566724
  5.6 99.7 %copy-start.3 = (s32[2,8192]{1,0:T(2,128)S(1)}, s32[2,8192]{1,0:T(2,128)}, u32[]{:S(2)}) copy-start(s32[2,8192]{1,0:T(2,128)} %member_ref.1) | copy-start | bytes 196612
